TPU v7x, 32 devices: a whole 2x2x4 slice. The times are simulated.
32 devices in a mesh: section: 4 (over x, core), tp: 8 (over z, y).
Axes of the slice: x: 2, y: 2, z: 4, core: 2. Of those that a mesh axis runs over, the one named last changes fastest.
Arguments:
- query: bfloat16 [4, 2, 1024, 4096], P('section', None, 'tp'), may hold values from -6 to 6
- keys_values: bfloat16 [4, 2, 2, 1024, 512], P('section', None, None, 'tp'), may hold values from -6 to 6
- grad_out: bfloat16 [4, 2, 1024, 4096], P('section', None, 'tp'), may hold values from -6 to 6
- fwd_query: bfloat16 [4, 2, 1024, 4096], P('section', None, 'tp'), may hold values from -6 to 6
- fwd_keys_values: bfloat16 [4, 2, 2, 1024, 512], P('section', None, None, 'tp'), may hold values from -6 to 6
- held_out: bfloat16 [4, 2, 1024, 4096], P('section', None, None, 'tp'), may hold values from -4 to 4
- evict: int32 [2, 2, 2], replicated, may hold values from 0 to 1
Outputs:
- passed_on: bfloat16 [4, 2, 1024, 4096], P('section', None, 'tp')
- grad_query: bfloat16 [4, 2, 1024, 4096], P('section', None, 'tp')
- grad_keys_values: bfloat16 [4, 2, 2, 1024, 512], P('section', None, None, 'tp')
- mirror_out: bfloat16 [4, 2, 1024, 4096], P('section', None, None, 'tp')
All inputs are finite; a program needn't handle non-finite values.
Results may differ from a plain program's by a relative error of at most 0.0057.
Values may be sent and summed in bfloat16 or wider, within the bound.
A program may use at most 128 MiB of HBM per device.

v0:
```python
import math

import jax
import jax.numpy as jnp
from jax import lax
from jax.experimental import pallas as pl
from jax.experimental.pallas import tpu as pltpu
from jax.sharding import PartitionSpec as P

HD = 128
MASKED = -1e30


def dot_nt(a, b):
    return lax.dot_general(a, b, (((1,), (1,)), ((), ())), preferred_element_type=jnp.float32)


def dot_nn(a, b):
    return lax.dot_general(a, b, (((1,), (0,)), ((), ())), preferred_element_type=jnp.float32)


def head_pair(ref, pair):
    first = ref[0, :, 2 * pair * HD : (2 * pair + 1) * HD]
    second = ref[0, :, (2 * pair + 1) * HD : (2 * pair + 2) * HD]
    return jnp.concatenate([first, second], axis=0)


def forward_kernel(pos_ref, q_ref, k_ref, v_ref, out_ref):
    rows = q_ref.shape[1]
    keys = k_ref[...].reshape(-1, HD)
    values = v_ref[...].reshape(-1, HD)
    seq = keys.shape[0]
    wide = jnp.concatenate([values, jnp.ones_like(values)], axis=1)
    row = lax.broadcasted_iota(jnp.int32, (2 * rows, seq), 0) % rows + pos_ref[0] * rows
    col = lax.broadcasted_iota(jnp.int32, (2 * rows, seq), 1)
    bias = jnp.where(col <= row, 0.0, MASKED)
    factor = math.log2(math.e) / math.sqrt(HD)
    for pair in range(q_ref.shape[2] // (2 * HD)):
        scores = dot_nt(head_pair(q_ref, pair), keys) * factor + bias
        top = jnp.max(scores, axis=1, keepdims=True)
        weights = jnp.exp2(scores - top).astype(jnp.bfloat16)
        total = dot_nn(weights, wide)
        out = (total[:, :HD] / total[:, HD:]).astype(out_ref.dtype)
        out_ref[0, :, 2 * pair * HD : (2 * pair + 1) * HD] = out[:rows]
        out_ref[0, :, (2 * pair + 1) * HD : (2 * pair + 2) * HD] = out[rows:]


def backward_kernel(
    pos_ref, flag_ref, q_ref, k_ref, v_ref, g_ref, *others
):
    *held_refs, dq_ref, dkv_ref = others
    rows = q_ref.shape[1]
    keys = k_ref[...].reshape(-1, HD)
    values = v_ref[...].reshape(-1, HD)
    seq = keys.shape[0]
    keys_t = keys.T
    row = lax.broadcasted_iota(jnp.int32, (seq, 2 * rows), 1) % rows + pos_ref[0] * rows
    col = lax.broadcasted_iota(jnp.int32, (seq, 2 * rows), 0)
    bias = jnp.where(col <= row, 0.0, MASKED)
    scale = 1.0 / math.sqrt(HD)
    factor = math.log2(math.e) * scale
    use_held = flag_ref[0] == 1
    dkeys = jnp.zeros((seq, HD), jnp.float32)
    dvalues = jnp.zeros((seq, HD), jnp.float32)
    pairs = q_ref.shape[2] // (2 * HD)
    for pair in range(pairs):
        queries = head_pair(q_ref, pair)
        grads = head_pair(g_ref, pair)
        each = pairs // len(held_refs)
        held = head_pair(held_refs[pair // each].at[0], pair % each)
        product = grads.astype(jnp.float32) * held.astype(jnp.float32)
        delta_held = jnp.sum(product.T, axis=0, keepdims=True)
        scores = dot_nt(keys, queries) * factor + bias
        top = jnp.max(scores, axis=0, keepdims=True)
        weights = jnp.exp2(scores - top)
        prob = weights * (1.0 / jnp.sum(weights, axis=0, keepdims=True))
        dprob = dot_nt(values, grads)
        delta_own = jnp.sum(prob * dprob, axis=0, keepdims=True)
        delta = jnp.where(use_held, delta_held, delta_own)
        dscore = (prob * (dprob - delta)).astype(jnp.bfloat16)
        dvalues = dvalues + dot_nn(prob.astype(jnp.bfloat16), grads)
        dkeys = dkeys + dot_nn(dscore, queries)
        dquery = (dot_nn(keys_t, dscore) * scale).T.astype(dq_ref.dtype)
        dq_ref[0, :, 2 * pair * HD : (2 * pair + 1) * HD] = dquery[:rows]
        dq_ref[0, :, (2 * pair + 1) * HD : (2 * pair + 2) * HD] = dquery[rows:]
    blocks = dkv_ref.shape[0]
    dkv_ref[:, 0] = (dkeys * scale).reshape(blocks, rows, HD).astype(dkv_ref.dtype)
    dkv_ref[:, 1] = dvalues.reshape(blocks, rows, HD).astype(dkv_ref.dtype)


PARAMS = pltpu.CompilerParams(vmem_limit_bytes=48 * 2**20)


def forward_all(position, query, gathered):
    micro, rows, width = query.shape
    blocks = gathered.shape[0]
    kv_count = gathered.shape[4] // HD
    group = width // kv_count
    kv_block = (blocks, 1, 1, rows, HD)
    work = micro * rows * width * blocks * rows
    return pl.pallas_call(
        forward_kernel,
        grid_spec=pltpu.PrefetchScalarGridSpec(
            num_scalar_prefetch=1,
            grid=(micro, kv_count),
            in_specs=[
                pl.BlockSpec((1, rows, group), lambda m, g, pos: (m, 0, g)),
                pl.BlockSpec(kv_block, lambda m, g, pos: (0, m, 0, 0, g)),
                pl.BlockSpec(kv_block, lambda m, g, pos: (0, m, 1, 0, g)),
            ],
            out_specs=pl.BlockSpec((1, rows, group), lambda m, g, pos: (m, 0, g)),
        ),
        out_shape=jax.ShapeDtypeStruct(query.shape, query.dtype),
        compiler_params=PARAMS,
        cost_estimate=pl.CostEstimate(
            flops=8 * work, bytes_accessed=12 * 2**20, transcendentals=work // HD
        ),
        name="attention_forward",
    )(position, query, gathered, gathered)


def backward_one(index, position, flag, query, gathered, grad, held):
    _, rows, width = query.shape
    blocks = gathered.shape[0]
    kv_count = gathered.shape[4] // HD
    group = width // kv_count
    kv_block = (blocks, 1, 1, rows, HD)
    token_block = pl.BlockSpec((1, rows, group), lambda g, pos, flag: (index, 0, g))
    held_block = (1, 1, rows, held.shape[3])
    parts = group // held.shape[3]

    def held_map(part):
        return lambda g, pos, flag: (lax.rem(pos[0] - parts * g - part + blocks, blocks), index, 0, 0)

    work = rows * width * blocks * rows
    return pl.pallas_call(
        backward_kernel,
        grid_spec=pltpu.PrefetchScalarGridSpec(
            num_scalar_prefetch=2,
            grid=(kv_count,),
            in_specs=[
                token_block,
                pl.BlockSpec(kv_block, lambda g, pos, flag: (0, index, 0, 0, g)),
                pl.BlockSpec(kv_block, lambda g, pos, flag: (0, index, 1, 0, g)),
                token_block,
            ]
            + [pl.BlockSpec(held_block, held_map(part)) for part in range(parts)],
            out_specs=[
                pl.BlockSpec((1, rows, group), lambda g, pos, flag: (0, 0, g)),
                pl.BlockSpec((blocks, 2, rows, HD), lambda g, pos, flag: (0, 0, 0, g)),
            ],
        ),
        out_shape=[
            jax.ShapeDtypeStruct((1, rows, width), query.dtype),
            jax.ShapeDtypeStruct((blocks, 2, rows, kv_count * HD), jnp.bfloat16),
        ],
        compiler_params=PARAMS,
        cost_estimate=pl.CostEstimate(
            flops=20 * work, bytes_accessed=12 * 2**20, transcendentals=work // HD
        ),
        name="attention_backward",
    )(position, flag, query, gathered, gathered, grad, *[held] * parts)


def per_device(query, keys_values, grad_out, fwd_query, fwd_keys_values, held_out, evict):
    query = query[0]
    keys_values = keys_values[0]
    grad_out = grad_out[0]
    fwd_query = fwd_query[0]
    fwd_keys_values = fwd_keys_values[0]
    held_local = held_out[0]
    sections = lax.axis_size("section")
    width = lax.axis_size("tp")
    half = sections // 2
    section_pos = lax.axis_index("section")
    tp_pos = lax.axis_index("tp")
    micro, rows = query.shape[:2]
    columns = held_local.shape[2]
    position = tp_pos.astype(jnp.int32).reshape(1)

    fwd_all = lax.all_gather(fwd_keys_values, "tp")
    bwd_all = lax.all_gather(keys_values, "tp")

    def to_mirror(chunk, turn, senders):
        route = [
            (s * width + t, (sections - 1 - s) * width + (t + turn) % width)
            for s in senders
            for t in range(width)
        ]
        return lax.ppermute(chunk, ("section", "tp"), route)

    held_parts = []
    for turn in range(width):
        start = (tp_pos + turn) % width * rows
        chunk = lax.dynamic_slice_in_dim(held_local, start, rows, 1)
        held_parts.append(to_mirror(chunk, turn, range(half, sections)))
    held = jnp.stack(held_parts)

    early = section_pos < half
    flag_pair = lax.dynamic_index_in_dim(
        evict, jnp.minimum(section_pos, half - 1), 0, keepdims=False
    )
    fwd_marked = jnp.logical_and(early, flag_pair[0] == 1)
    bwd_marked = jnp.logical_and(early, flag_pair[1] == 1).astype(jnp.int32)

    out = forward_all(position, fwd_query, fwd_all)
    passed = lax.ppermute(out, "section", [(s, s + 1) for s in range(sections - 1)])
    mirror = jnp.zeros((micro, width * rows, columns), out.dtype)
    for turn in range(width):
        start = (tp_pos + turn) % width * columns
        chunk = lax.dynamic_slice_in_dim(out, start, columns, 2)
        chunk = jnp.where(fwd_marked[:, None, None], chunk, jnp.zeros_like(chunk))
        arrived = to_mirror(chunk, turn, range(half))
        place = (tp_pos - turn + width) % width * rows
        mirror = lax.dynamic_update_slice_in_dim(mirror, arrived, place, 1)

    dqs = []
    grads = []
    for index in range(micro):
        dquery, partial = backward_one(
            index, position, bwd_marked[index : index + 1], query, bwd_all, grad_out, held
        )
        dqs.append(dquery)
        grads.append(lax.psum_scatter(partial, "tp", scatter_dimension=0))
    return (passed[None], jnp.concatenate(dqs)[None], jnp.stack(grads)[None], mirror[None])


def solution(mesh):
    return jax.shard_map(
        per_device,
        mesh=mesh,
        in_specs=(
            P("section", None, "tp", None),
            P("section", None, None, "tp", None),
            P("section", None, "tp", None),
            P("section", None, "tp", None),
            P("section", None, None, "tp", None),
            P("section", None, None, "tp"),
            P(),
        ),
        out_specs=(
            P("section", None, "tp", None),
            P("section", None, "tp", None),
            P("section", None, None, "tp", None),
            P("section", None, None, "tp"),
        ),
        check_vma=False,
    )
```

profile of v0, /device:TPU:26, one launch (start us, length us, event | category | flops | bytes accessed | tf_op | source)
XLA Modules:
  0.0 371.7 jit_solution(10946353019896000997)
XLA Ops:
  8.8 2.5 dynamic-slice_bitcast_fusion
  11.3 1.9 collective-permute-start.1
  13.2 3.0 collective-permute-start.2
  16.2 2.0 collective-permute-start.3
  18.2 2.0 collective-permute-start.4
  20.2 2.0 collective-permute-start.5
  23.5 9.2 %collective-permute-start.6 = (bf16[2,128,512]{2,1,0:T(8,128)(2,1)S(1)}, bf16[2,128,512]{2,1,0:T(8,128)(2,1)S(1)}, u32[]{:S(2)}, u32[]{:S(2)}) collective-permute-start(bf16[2,128,512]{2,1,0:T(8,128)(2,1)S(1)} %get-tuple-element.21), channel_id=1, source_target_pairs={{16,13},{17,14},{18,15},{19,8},{20,9},{21,10},{22,11},{23,12},{24,... | collective-permute-start | bytes 786440 | tf_op jit(solution)/shard_map/ppermute | solution.py:190
  32.7 1.7 bitcast_dynamic-update-slice_fusion.15
  34.4 1.3 collective-permute-start.7
  35.7 1.7 bitcast_dynamic-update-slice_fusion.14
  37.4 29.6 %collective-permute-start.8 = (bf16[2,128,512]{2,1,0:T(8,128)(2,1)S(1)}, bf16[2,128,512]{2,1,0:T(8,128)(2,1)S(1)}, u32[]{:S(2)}, u32[]{:S(2)}) collective-permute-start(bf16[2,128,512]{2,1,0:T(8,128)(2,1)S(1)} %get-tuple-element.20), channel_id=1, source_target_pairs={{16,15},{17,8},{18,9},{19,10},{20,11},{21,12},{22,13},{23,14},{24,... | collective-permute-start | bytes 786440 | tf_op jit(solution)/shard_map/ppermute | solution.py:190
  67.0 1.7 bitcast_dynamic-update-slice_fusion.13
  68.7 1.7 bitcast_dynamic-update-slice_fusion.12
  70.4 1.7 bitcast_dynamic-update-slice_fusion.11
  74.2 41.6 %all-gather.5.cloned.1.call-done.k_ref.v_ref = bf16[8,2,2,128,512]{4,3,2,1,0:T(8,128)(2,1)} async-done(((bf16[1,2,2,128,512]{4,3,2,1,0:T(8,128)(2,1)}), bf16[8,2,2,128,512]{4,3,2,1,0:T(8,128)(2,1)}) %all-gather.5.cloned.1.call-update) | async-done | bytes 4194320 | tf_op jit(solution)/shard_map/all_gather | solution.py:182
  115.8 21.9 %attention_backward.2 = (bf16[1,128,4096]{2,1,0:T(8,128)(2,1)S(1)}, bf16[8,2,128,512]{3,2,1,0:T(8,128)(2,1)}) custom-call(s32[1]{0:T(128)} %bitcast.pos_ref, s32[1]{0:T(128)} %bitcast.3.flag_ref, bf16[2,128,4096]{2,1,0:T(8,128)(2,1)S(1)} %bitcast.61, bf16[8,2,2,128,512]{4,3,2,1,0:T(8,128)(2,1)} %all-gather.5.cloned.1.call-done.k_ref.v_ref, ...), custom_call_target="tpu_custom_call" | custom-call | flops 10737418240 | bytes 12582912 | tf_op jit(solution)/shard_map/attention_backward/pallas_call | solution.py:136
  138.0 1.6 copy-done.2
  139.6 21.9 %attention_backward.3 = (bf16[1,128,4096]{2,1,0:T(8,128)(2,1)S(1)}, bf16[8,2,128,512]{3,2,1,0:T(8,128)(2,1)}) custom-call(s32[1]{0:T(128)} %bitcast.pos_ref, s32[1]{0:T(128)} %bitcast.22.flag_ref, bf16[2,128,4096]{2,1,0:T(8,128)(2,1)S(1)} %bitcast.62, bf16[8,2,2,128,512]{4,3,2,1,0:T(8,128)(2,1)} %all-gather.5.cloned.1.call-done.k_ref.v_ref, ...), custom_call_target="tpu_custom_call" | custom-call | flops 10737418240 | bytes 12582912 | tf_op jit(solution)/shard_map/attention_backward/pallas_call | solution.py:136
  161.6 30.7 %all-gather.3.cloned.1.call-done.k_ref.v_ref = bf16[8,2,2,128,512]{4,3,2,1,0:T(8,128)(2,1)} async-done(((bf16[1,2,2,128,512]{4,3,2,1,0:T(8,128)(2,1)}), bf16[8,2,2,128,512]{4,3,2,1,0:T(8,128)(2,1)}) %all-gather.3.cloned.1.call-update) | async-done | bytes 4194320 | tf_op jit(solution)/shard_map/all_gather | solution.py:181
  192.3 1.6 copy-done.3
  193.9 16.3 %attention_forward.1 = bf16[2,128,4096]{2,1,0:T(8,128)(2,1)S(1)} custom-call(s32[1]{0:T(128)} %bitcast.pos_ref, bf16[2,128,4096]{2,1,0:T(8,128)(2,1)S(1)} %bitcast.63, bf16[8,2,2,128,512]{4,3,2,1,0:T(8,128)(2,1)} %all-gather.3.cloned.1.call-done.k_ref.v_ref, bf16[8,2,2,128,512]{4,3,2,1,0:T(8,128)(2,1)} %all-gather.3.cloned.1.call-done.k_ref.v_ref), custom_call_target="tpu_custom_call" | custom-call | flops 8589934592 | bytes 12582912 | tf_op jit(solution)/shard_map/attention_forward/pallas_call | solution.py:101
  210.1 1.9 collective-permute-start
  213.1 1.3 collective-permute-start.9
  214.4 1.3 collective-permute-start.10
  218.3 1.5 maximum_bitcast_fusion
  219.8 48.7 %collective-permute-done.9 = bf16[2,128,512]{2,1,0:T(8,128)(2,1)S(1)} collective-permute-done((bf16[2,128,512]{2,1,0:T(8,128)(2,1)S(1)}, bf16[2,128,512]{2,1,0:T(8,128)(2,1)S(1)}, u32[]{:S(2)}, u32[]{:S(2)}) %collective-permute-start.9) | collective-permute-done | bytes 262176 | tf_op jit(solution)/shard_map/ppermute | solution.py:190
  269.9 1.3 collective-permute-start.14
  273.9 17.3 %collective-permute-done.13 = bf16[2,128,512]{2,1,0:T(8,128)(2,1)S(1)} collective-permute-done((bf16[2,128,512]{2,1,0:T(8,128)(2,1)S(1)}, bf16[2,128,512]{2,1,0:T(8,128)(2,1)S(1)}, u32[]{:S(2)}, u32[]{:S(2)}) %collective-permute-start.13) | collective-permute-done | bytes 262176 | tf_op jit(solution)/shard_map/ppermute | solution.py:190
  291.8 1.4 copy-done.5
  293.1 67.0 %reduce-scatter.5.cloned.1.call-done = bf16[1,2,128,512]{3,2,1,0:T(8,128)(2,1)} async-done(((bf16[8,2,128,512]{3,2,1,0:T(8,128)(2,1)}), bf16[1,2,128,512]{3,2,1,0:T(8,128)(2,1)}) %reduce-scatter.5.cloned.1.call-update) | async-done | bytes 262160 | tf_op jit(solution)/shard_map/reduce_scatter | solution.py:224
  360.1 1.9 maximum_bitcast_fusion.1
  362.0 3.1 copy.27
  (56 shorter events, 13.4 us)
Async XLA Ops:
  7.2 15.0 %copy-start = (s32[2,2,2]{2,1,0:T(2,128)S(1)}, s32[2,2,2]{2,1,0:T(2,128)}, u32[]{:S(2)}) copy-start(s32[2,2,2]{2,1,0:T(2,128)} %param.13) | copy-start | bytes 100
  7.2 108.6 %all-gather.5.cloned.1.call-start = ((), (), s32[]{:S(2)}) async-start(), calls=%async_computation.3 | async-start | bytes 4718592 | tf_op jit(solution)/shard_map/all_gather | solution.py:182
  7.9 184.4 %all-gather.3.cloned.1.call-start = ((), (), s32[]{:S(2)}) async-start(), calls=%async_computation.2 | async-start | bytes 4718592 | tf_op jit(solution)/shard_map/all_gather | solution.py:181
  8.7 284.5 %reduce-scatter.3.cloned.1.call-start = ((), (), s32[]{:S(2)}) async-start(), calls=%async_computation.4 | async-start | bytes 2359296 | tf_op jit(solution)/shard_map/reduce_scatter | solution.py:224
  11.3 11.5 %collective-permute-start.1 = (bf16[2,128,512]{2,1,0:T(8,128)(2,1)S(1)}, bf16[2,128,512]{2,1,0:T(8,128)(2,1)S(1)}, u32[]{:S(2)}, u32[]{:S(2)}) collective-permute-start(bf16[2,128,512]{2,1,0:T(8,128)(2,1)S(1)} %get-tuple-element.26), channel_id=1, source_target_pairs={{16,8},{17,9},{18,10},{19,11},{20,12},{21,13},{22,14},{23,15},{24,... | collective-permute-start | bytes 786440 | tf_op jit(solution)/shard_map/ppermute | solution.py:190
  13.2 21.2 %collective-permute-start.2 = (bf16[2,128,512]{2,1,0:T(8,128)(2,1)}, bf16[2,128,512]{2,1,0:T(8,128)(2,1)}, u32[]{:S(2)}, u32[]{:S(2)}) collective-permute-start(bf16[2,128,512]{2,1,0:T(8,128)(2,1)} %get-tuple-element.25), channel_id=1, source_target_pairs={{16,9},{17,10},{18,11},{19,12},{20,13},{21,14},{22,15},{23,8},{24,... | collective-permute-start | bytes 786440 | tf_op jit(solution)/shard_map/ppermute | solution.py:190
  16.2 21.2 %collective-permute-start.3 = (bf16[2,128,512]{2,1,0:T(8,128)(2,1)}, bf16[2,128,512]{2,1,0:T(8,128)(2,1)}, u32[]{:S(2)}, u32[]{:S(2)}) collective-permute-start(bf16[2,128,512]{2,1,0:T(8,128)(2,1)} %get-tuple-element.24), channel_id=1, source_target_pairs={{16,10},{17,11},{18,12},{19,13},{20,14},{21,15},{22,8},{23,9},{24,... | collective-permute-start | bytes 786440 | tf_op jit(solution)/shard_map/ppermute | solution.py:190
  18.2 50.5 %collective-permute-start.4 = (bf16[2,128,512]{2,1,0:T(8,128)(2,1)S(1)}, bf16[2,128,512]{2,1,0:T(8,128)(2,1)}, u32[]{:S(2)}, u32[]{:S(2)}) collective-permute-start(bf16[2,128,512]{2,1,0:T(8,128)(2,1)S(1)} %get-tuple-element.23), channel_id=1, source_target_pairs={{16,11},{17,12},{18,13},{19,14},{20,15},{21,8},{22,9},{23,10},{24,... | collective-permute-start | bytes 786440 | tf_op jit(solution)/shard_map/ppermute | solution.py:190
  20.2 50.2 %collective-permute-start.5 = (bf16[2,128,512]{2,1,0:T(8,128)(2,1)S(1)}, bf16[2,128,512]{2,1,0:T(8,128)(2,1)}, u32[]{:S(2)}, u32[]{:S(2)}) collective-permute-start(bf16[2,128,512]{2,1,0:T(8,128)(2,1)S(1)} %get-tuple-element.22), channel_id=1, source_target_pairs={{16,12},{17,13},{18,14},{19,15},{20,8},{21,9},{22,10},{23,11},{24,... | collective-permute-start | bytes 786440 | tf_op jit(solution)/shard_map/ppermute | solution.py:190
  22.8 0.7 copy-start.6
  23.5 92.3 %copy-start.1 = (bf16[1,2,128,4096]{3,2,1,0:T(8,128)(2,1)S(1)}, bf16[1,2,128,4096]{3,2,1,0:T(8,128)(2,1)}, u32[]{:S(2)}) copy-start(bf16[1,2,128,4096]{3,2,1,0:T(8,128)(2,1)} %param.7) | copy-start | bytes 6291460
  23.5 48.5 %collective-permute-start.6 = (bf16[2,128,512]{2,1,0:T(8,128)(2,1)S(1)}, bf16[2,128,512]{2,1,0:T(8,128)(2,1)S(1)}, u32[]{:S(2)}, u32[]{:S(2)}) collective-permute-start(bf16[2,128,512]{2,1,0:T(8,128)(2,1)S(1)} %get-tuple-element.21), channel_id=1, source_target_pairs={{16,13},{17,14},{18,15},{19,8},{20,9},{21,10},{22,11},{23,12},{24,... | collective-permute-start | bytes 786440 | tf_op jit(solution)/shard_map/ppermute | solution.py:190
  34.4 38.4 %collective-permute-start.7 = (bf16[2,128,512]{2,1,0:T(8,128)(2,1)S(1)}, bf16[2,128,512]{2,1,0:T(8,128)(2,1)S(1)}, u32[]{:S(2)}, u32[]{:S(2)}) collective-permute-start(bf16[2,128,512]{2,1,0:T(8,128)(2,1)S(1)} %get-tuple-element.27), channel_id=1, source_target_pairs={{16,14},{17,15},{18,8},{19,9},{20,10},{21,11},{22,12},{23,13},{24,... | collective-permute-start | bytes 786440 | tf_op jit(solution)/shard_map/ppermute | solution.py:190
  37.4 36.1 %collective-permute-start.8 = (bf16[2,128,512]{2,1,0:T(8,128)(2,1)S(1)}, bf16[2,128,512]{2,1,0:T(8,128)(2,1)S(1)}, u32[]{:S(2)}, u32[]{:S(2)}) collective-permute-start(bf16[2,128,512]{2,1,0:T(8,128)(2,1)S(1)} %get-tuple-element.20), channel_id=1, source_target_pairs={{16,15},{17,8},{18,9},{19,10},{20,11},{21,12},{22,13},{23,14},{24,... | collective-permute-start | bytes 786440 | tf_op jit(solution)/shard_map/ppermute | solution.py:190
  137.7 222.4 %reduce-scatter.5.cloned.1.call-start = ((), (), s32[]{:S(2)}) async-start(), calls=%async_computation.5 | async-start | bytes 2359296 | tf_op jit(solution)/shard_map/reduce_scatter | solution.py:224
  138.0 1.6 copy-start.2
  192.3 1.6 copy-start.3
  210.1 81.6 %collective-permute-start = (bf16[2,128,4096]{2,1,0:T(8,128)(2,1)S(1)}, bf16[2,128,4096]{2,1,0:T(8,128)(2,1)S(1)}, u32[]{:S(2)}, u32[]{:S(2)}) collective-permute-start(bf16[2,128,4096]{2,1,0:T(8,128)(2,1)S(1)} %attention_forward.1), channel_id=1, source_target_pairs={{0,8},{8,16},{16,24},{1,9},{9,17},{17,25},{2,10},{10,18},{18,26},{... | collective-permute-start | bytes 6291464 | tf_op jit(solution)/shard_map/ppermute | solution.py:207
  213.1 55.4 %collective-permute-start.9 = (bf16[2,128,512]{2,1,0:T(8,128)(2,1)S(1)}, bf16[2,128,512]{2,1,0:T(8,128)(2,1)S(1)}, u32[]{:S(2)}, u32[]{:S(2)}) collective-permute-start(bf16[2,128,512]{2,1,0:T(8,128)(2,1)S(1)} %get-tuple-element.19), channel_id=1, source_target_pairs={{0,24},{1,25},{2,26},{3,27},{4,28},{5,29},{6,30},{7,31},{8,16},{9,... | collective-permute-start | bytes 786440 | tf_op jit(solution)/shard_map/ppermute | solution.py:190
  214.4 55.5 %collective-permute-start.10 = (bf16[2,128,512]{2,1,0:T(8,128)(2,1)S(1)}, bf16[2,128,512]{2,1,0:T(8,128)(2,1)S(1)}, u32[]{:S(2)}, u32[]{:S(2)}) collective-permute-start(bf16[2,128,512]{2,1,0:T(8,128)(2,1)S(1)} %get-tuple-element.18), channel_id=1, source_target_pairs={{0,25},{1,26},{2,27},{3,28},{4,29},{5,30},{6,31},{7,24},{8,17},{9,... | collective-permute-start | bytes 786440 | tf_op jit(solution)/shard_map/ppermute | solution.py:190
  215.7 55.6 %collective-permute-start.11 = (bf16[2,128,512]{2,1,0:T(8,128)(2,1)S(1)}, bf16[2,128,512]{2,1,0:T(8,128)(2,1)S(1)}, u32[]{:S(2)}, u32[]{:S(2)}) collective-permute-start(bf16[2,128,512]{2,1,0:T(8,128)(2,1)S(1)} %get-tuple-element.17), channel_id=1, source_target_pairs={{0,26},{1,27},{2,28},{3,29},{4,30},{5,31},{6,24},{7,25},{8,18},{9,... | collective-permute-start | bytes 786440 | tf_op jit(solution)/shard_map/ppermute | solution.py:190
  217.0 55.6 %collective-permute-start.12 = (bf16[2,128,512]{2,1,0:T(8,128)(2,1)S(1)}, bf16[2,128,512]{2,1,0:T(8,128)(2,1)S(1)}, u32[]{:S(2)}, u32[]{:S(2)}) collective-permute-start(bf16[2,128,512]{2,1,0:T(8,128)(2,1)S(1)} %get-tuple-element.16), channel_id=1, source_target_pairs={{0,27},{1,28},{2,29},{3,30},{4,31},{5,24},{6,25},{7,26},{8,19},{9,... | collective-permute-start | bytes 786440 | tf_op jit(solution)/shard_map/ppermute | solution.py:190
  268.4 22.8 %collective-permute-start.13 = (bf16[2,128,512]{2,1,0:T(8,128)(2,1)S(1)}, bf16[2,128,512]{2,1,0:T(8,128)(2,1)S(1)}, u32[]{:S(2)}, u32[]{:S(2)}) collective-permute-start(bf16[2,128,512]{2,1,0:T(8,128)(2,1)S(1)} %get-tuple-element.15), channel_id=1, source_target_pairs={{0,28},{1,29},{2,30},{3,31},{4,24},{5,25},{6,26},{7,27},{8,20},{9,... | collective-permute-start | bytes 786440 | tf_op jit(solution)/shard_map/ppermute | solution.py:190
  269.9 21.4 %collective-permute-start.14 = (bf16[2,128,512]{2,1,0:T(8,128)(2,1)S(1)}, bf16[2,128,512]{2,1,0:T(8,128)(2,1)S(1)}, u32[]{:S(2)}, u32[]{:S(2)}) collective-permute-start(bf16[2,128,512]{2,1,0:T(8,128)(2,1)S(1)} %get-tuple-element.14), channel_id=1, source_target_pairs={{0,29},{1,30},{2,31},{3,24},{4,25},{5,26},{6,27},{7,28},{8,21},{9,... | collective-permute-start | bytes 786440 | tf_op jit(solution)/shard_map/ppermute | solution.py:190
  271.3 20.1 %collective-permute-start.15 = (bf16[2,128,512]{2,1,0:T(8,128)(2,1)S(1)}, bf16[2,128,512]{2,1,0:T(8,128)(2,1)S(1)}, u32[]{:S(2)}, u32[]{:S(2)}) collective-permute-start(bf16[2,128,512]{2,1,0:T(8,128)(2,1)S(1)} %get-tuple-element.13), channel_id=1, source_target_pairs={{0,30},{1,31},{2,24},{3,25},{4,26},{5,27},{6,28},{7,29},{8,22},{9,... | collective-permute-start | bytes 786440 | tf_op jit(solution)/shard_map/ppermute | solution.py:190
  272.6 19.1 %collective-permute-start.16 = (bf16[2,128,512]{2,1,0:T(8,128)(2,1)S(1)}, bf16[2,128,512]{2,1,0:T(8,128)(2,1)S(1)}, u32[]{:S(2)}, u32[]{:S(2)}) collective-permute-start(bf16[2,128,512]{2,1,0:T(8,128)(2,1)S(1)} %get-tuple-element.12), channel_id=1, source_target_pairs={{0,31},{1,24},{2,25},{3,26},{4,27},{5,28},{6,29},{7,30},{8,23},{9,... | collective-permute-start | bytes 786440 | tf_op jit(solution)/shard_map/ppermute | solution.py:190
  291.7 73.4 %copy-start.4 = (bf16[1,2,1024,512]{3,2,1,0:T(8,128)(2,1)}, bf16[1,2,1024,512]{3,2,1,0:T(8,128)(2,1)S(1)}, u32[]{:S(2)}) copy-start(bf16[1,2,1024,512]{3,2,1,0:T(8,128)(2,1)S(1)} %bitcast_dynamic-update-slice_fusion) | copy-start | bytes 6291460
  291.8 1.4 copy-start.5
Sparse Core Ops, SparseCore 0:
  10.1 105.5 all-gather.4
  117.9 74.3 all-gather.2
  195.8 83.4 reduce-scatter.2
  283.2 76.8 reduce-scatter.4
where the time goes:
time: 376 us; the launch traced here: 372 us
  waiting for transfers between devices  207 us (55%)
  starting transfers between devices  63.5 us (17%)
  Pallas kernels  60.1 us (16%)
  local copies, waits for them, and re-layouts  22.4 us (6%)
  between operations  14.2 us (4%)
  other arithmetic  4.37 us (1%)
    reduce_scatter x2, waiting for transfers between devices, per_device(): grads.append(lax.psum_scatter(partial, 'tp', scatter_dimension=0))  67 us
    ppermute x16, waiting for transfers between devices, to_mirror(): return lax.ppermute(chunk, ('section', 'tp'), route)  66.4 us
    ppermute x16, starting transfers between devices, to_mirror(): return lax.ppermute(chunk, ('section', 'tp'), route)  61.3 us
    pallas_call x2, Pallas kernels, backward_one(): pl.pallas_call(backward_kernel, grid_spec=pltpu.PrefetchScalarGridSpec(nu...  43.8 us
    all_gather x1, waiting for transfers between devices, per_device(): bwd_all = lax.all_gather(keys_values, 'tp')  41.6 us
    all_gather x1, waiting for transfers between devices, per_device(): fwd_all = lax.all_gather(fwd_keys_values, 'tp')  30.7 us
    unnamed x22, local copies, waits for them, and re-layouts  18.2 us
    pallas_call x1, Pallas kernels, forward_all(): pl.pallas_call(forward_kernel, grid_spec=pltpu.PrefetchScalarGridSpec(num...  16.3 us
  transfers between devices with their start and end apart: 21, of which 6 were waited for; matrix products, arithmetic and copies ran while one was open for 4% of the time, Pallas kernels for 16%

commit v1 on v0

--- a/solution.py
+++ b/solution.py
@@ -25,13 +25,13 @@
     return jnp.concatenate([first, second], axis=0)
 
 
-def forward_kernel(pos_ref, q_ref, k_ref, v_ref, out_ref):
+def attend_block(position, q_ref, k_ref, v_ref, out_ref):
     rows = q_ref.shape[1]
     keys = k_ref[...].reshape(-1, HD)
     values = v_ref[...].reshape(-1, HD)
     seq = keys.shape[0]
     wide = jnp.concatenate([values, jnp.ones_like(values)], axis=1)
-    row = lax.broadcasted_iota(jnp.int32, (2 * rows, seq), 0) % rows + pos_ref[0] * rows
+    row = lax.broadcasted_iota(jnp.int32, (2 * rows, seq), 0) % rows + position * rows
     col = lax.broadcasted_iota(jnp.int32, (2 * rows, seq), 1)
     bias = jnp.where(col <= row, 0.0, MASKED)
     factor = math.log2(math.e) / math.sqrt(HD)
@@ -43,6 +43,241 @@
         out = (total[:, :HD] / total[:, HD:]).astype(out_ref.dtype)
         out_ref[0, :, 2 * pair * HD : (2 * pair + 1) * HD] = out[:rows]
         out_ref[0, :, (2 * pair + 1) * HD : (2 * pair + 2) * HD] = out[rows:]
+
+
+def neighbours():
+    me = lax.axis_index("tp")
+    width = lax.axis_size("tp")
+    level = me // 2
+    pair = me + 1 - 2 * (me % 2)
+    return me, level, width // 2, pair, (me + 2) % width, (me + width - 2) % width
+
+
+def greet():
+    _, level, levels, pair, up, down = neighbours()
+    barrier = pltpu.get_barrier_semaphore()
+    pl.semaphore_signal(barrier, inc=1, device_id={"tp": pair})
+
+    @pl.when(level < levels - 1)
+    def _():
+        pl.semaphore_signal(barrier, inc=1, device_id={"tp": up})
+
+    @pl.when(level > 0)
+    def _():
+        pl.semaphore_signal(barrier, inc=1, device_id={"tp": down})
+
+    peers = 1 + jnp.minimum(level, 1) + jnp.minimum(levels - 1 - level, 1)
+    pl.semaphore_wait(barrier, peers)
+
+
+class Gather:
+    def __init__(self, shard, full, sems):
+        self.shard, self.full = shard, full
+        self.local, self.up_send, self.up_recv, self.pair_send, self.pair_recv = sems
+        self.me, self.level, self.levels, self.pair, self.up, _ = neighbours()
+        self.micro = shard.shape[0]
+
+    def copy(self, step, m, source, sends, recvs, target):
+        first = self.me if source is None else source
+        src = self.shard.at[m] if step == 0 and source is None else self.full.at[first - 2 * step, m]
+        return pltpu.make_async_remote_copy(
+            src_ref=src,
+            dst_ref=self.full.at[first - 2 * step, m],
+            send_sem=sends.at[step, m],
+            recv_sem=recvs.at[step, m],
+            device_id={"tp": target},
+        )
+
+    def to_up(self, step, m):
+        return self.copy(step, m, None, self.up_send, self.up_recv, self.up)
+
+    def from_down(self, step, m):
+        return self.copy(step, m, self.me - 2, self.up_send, self.up_recv, self.up)
+
+    def to_pair(self, step, m):
+        return self.copy(step, m, None, self.pair_send, self.pair_recv, self.pair)
+
+    def from_pair(self, step, m):
+        return self.copy(step, m, self.pair, self.pair_send, self.pair_recv, self.pair)
+
+    def fill(self, action):
+        for place in range(2 * self.levels):
+
+            @pl.when(jnp.logical_or(place == self.me, place // 2 > self.level))
+            def _():
+                copy = pltpu.make_async_copy(self.shard, self.full.at[place], self.local.at[place])
+                copy.start() if action == "start" else copy.wait()
+
+    def step(self, step):
+        for m in range(self.micro):
+
+            @pl.when(self.level >= step)
+            def _():
+                if step > 0:
+                    self.from_down(step - 1, m).wait_recv()
+
+                @pl.when(self.level < self.levels - 1)
+                def _():
+                    self.to_up(step, m).start()
+
+                self.to_pair(step, m).start()
+
+        if step == 0:
+            self.fill("start")
+
+    def finish(self):
+        for step in range(self.levels):
+            for m in range(self.micro):
+
+                @pl.when(self.level >= step)
+                def _():
+                    self.from_pair(step, m).wait_recv()
+                    self.to_pair(step, m).wait_send()
+
+                    @pl.when(self.level < self.levels - 1)
+                    def _():
+                        self.to_up(step, m).wait_send()
+
+        self.fill("wait")
+
+
+def gather_scratch(micro):
+    width = lax.axis_size("tp")
+    steps = pltpu.SemaphoreType.DMA((width // 2, micro))
+    return [pltpu.SemaphoreType.DMA((width,)), steps, steps, steps, steps]
+
+
+def gather_kernel(shard_ref, full_ref, *sems):
+    greet()
+    gather = Gather(shard_ref, full_ref, sems)
+    for step in range(gather.levels):
+        gather.step(step)
+    gather.finish()
+
+
+def gather_all(shard):
+    full = (lax.axis_size("tp"),) + shard.shape
+    return pl.pallas_call(
+        gather_kernel,
+        in_specs=[pl.BlockSpec(memory_space=pl.ANY)],
+        out_specs=pl.BlockSpec(memory_space=pl.ANY),
+        out_shape=jax.ShapeDtypeStruct(full, shard.dtype),
+        scratch_shapes=gather_scratch(shard.shape[0]),
+        compiler_params=pltpu.CompilerParams(collective_id=0, has_side_effects=True),
+        name="gather_keys_values",
+    )(shard)
+
+
+def forward_kernel(q_ref, k_ref, v_ref, shard_ref, out_ref, full_ref, *sems):
+    now = pl.program_id(0) * pl.num_programs(1) + pl.program_id(1)
+    micro = shard_ref.shape[0]
+    total = micro * (shard_ref.shape[3] // HD)
+    gather = Gather(shard_ref, full_ref, sems)
+
+    @pl.when(now == 0)
+    def _():
+        greet()
+
+    for step in range(gather.levels):
+
+        @pl.when(now == step * total // gather.levels)
+        def _():
+            gather.step(step)
+
+    attend_block(gather.me, q_ref, k_ref, v_ref, out_ref)
+
+    @pl.when(now == total - 1)
+    def _():
+        gather.finish()
+
+
+def scatter_kernel(*refs):
+    (
+        *parts, out_ref, pair_in, up_in, staged, total,
+        pair_send, pair_recv, down_send, down_recv,
+    ) = refs
+    me, level, levels, pair, _, down = neighbours()
+    side = me % 2
+    micro = len(parts)
+    greet()
+
+    def to_pair(place, m):
+        return pltpu.make_async_remote_copy(
+            src_ref=parts[m].at[2 * place + 1 - side],
+            dst_ref=pair_in.at[place, m],
+            send_sem=pair_send.at[place, m],
+            recv_sem=pair_recv.at[place, m],
+            device_id={"tp": pair},
+        )
+
+    def to_down(place, m):
+        return pltpu.make_async_remote_copy(
+            src_ref=staged.at[place, m],
+            dst_ref=up_in.at[place, m],
+            send_sem=down_send.at[place, m],
+            recv_sem=down_recv.at[place, m],
+            device_id={"tp": down},
+        )
+
+    for place in range(levels):
+        for m in range(micro):
+
+            @pl.when(level >= place)
+            def _():
+                to_pair(place, m).start()
+
+    for place in range(levels):
+        for m in range(micro):
+
+            @pl.when(level >= place)
+            def _():
+                to_pair(place, m).wait_recv()
+                own = parts[m][2 * place + side].astype(jnp.float32)
+                total[...] = own + pair_in[place, m].astype(jnp.float32)
+
+                @pl.when(level < levels - 1)
+                def _():
+                    to_down(place, m).wait_recv()
+                    total[...] += up_in[place, m].astype(jnp.float32)
+
+                @pl.when(level > place)
+                def _():
+                    staged[place, m] = total[...].astype(staged.dtype)
+                    to_down(place, m).start()
+
+                @pl.when(level == place)
+                def _():
+                    out_ref[m] = total[...].astype(out_ref.dtype)
+
+    for place in range(levels):
+        for m in range(micro):
+
+            @pl.when(level >= place)
+            def _():
+                to_pair(place, m).wait_send()
+
+            @pl.when(level > place)
+            def _():
+                to_down(place, m).wait_send()
+
+
+def scatter_sum(parts):
+    micro = len(parts)
+    levels = parts[0].shape[0] // 2
+    block = parts[0].shape[1:]
+    slots = pltpu.VMEM((levels, micro) + block, jnp.bfloat16)
+    steps = pltpu.SemaphoreType.DMA((levels, micro))
+    return pl.pallas_call(
+        scatter_kernel,
+        in_specs=[pl.BlockSpec(memory_space=pltpu.VMEM)] * micro,
+        out_specs=pl.BlockSpec(memory_space=pltpu.VMEM),
+        out_shape=jax.ShapeDtypeStruct((micro,) + block, jnp.bfloat16),
+        scratch_shapes=[slots, slots, slots, pltpu.VMEM(block, jnp.float32)] + [steps] * 4,
+        compiler_params=pltpu.CompilerParams(
+            collective_id=2, has_side_effects=True, vmem_limit_bytes=32 * 2**20
+        ),
+        name="scatter_gradients",
+    )(*parts)
 
 
 def backward_kernel(
@@ -91,7 +326,7 @@
 PARAMS = pltpu.CompilerParams(vmem_limit_bytes=48 * 2**20)
 
 
-def forward_all(position, query, gathered):
+def forward_all(query, gathered, shard):
     micro, rows, width = query.shape
     blocks = gathered.shape[0]
     kv_count = gathered.shape[4] // HD
@@ -100,23 +335,30 @@
     work = micro * rows * width * blocks * rows
     return pl.pallas_call(
         forward_kernel,
-        grid_spec=pltpu.PrefetchScalarGridSpec(
-            num_scalar_prefetch=1,
-            grid=(micro, kv_count),
-            in_specs=[
-                pl.BlockSpec((1, rows, group), lambda m, g, pos: (m, 0, g)),
-                pl.BlockSpec(kv_block, lambda m, g, pos: (0, m, 0, 0, g)),
-                pl.BlockSpec(kv_block, lambda m, g, pos: (0, m, 1, 0, g)),
-            ],
-            out_specs=pl.BlockSpec((1, rows, group), lambda m, g, pos: (m, 0, g)),
-        ),
-        out_shape=jax.ShapeDtypeStruct(query.shape, query.dtype),
-        compiler_params=PARAMS,
+        grid=(micro, kv_count),
+        in_specs=[
+            pl.BlockSpec((1, rows, group), lambda m, g: (m, 0, g)),
+            pl.BlockSpec(kv_block, lambda m, g: (0, m, 0, 0, g)),
+            pl.BlockSpec(kv_block, lambda m, g: (0, m, 1, 0, g)),
+            pl.BlockSpec(memory_space=pl.ANY),
+        ],
+        out_specs=[
+            pl.BlockSpec((1, rows, group), lambda m, g: (m, 0, g)),
+            pl.BlockSpec(memory_space=pl.ANY),
+        ],
+        out_shape=[
+            jax.ShapeDtypeStruct(query.shape, query.dtype),
+            jax.ShapeDtypeStruct((blocks,) + shard.shape, shard.dtype),
+        ],
+        scratch_shapes=gather_scratch(micro),
+        compiler_params=pltpu.CompilerParams(
+            collective_id=1, has_side_effects=True, vmem_limit_bytes=48 * 2**20
+        ),
         cost_estimate=pl.CostEstimate(
             flops=8 * work, bytes_accessed=12 * 2**20, transcendentals=work // HD
         ),
         name="attention_forward",
-    )(position, query, gathered, gathered)
+    )(query, gathered, gathered, shard)
 
 
 def backward_one(index, position, flag, query, gathered, grad, held):
@@ -178,8 +420,7 @@
     columns = held_local.shape[2]
     position = tp_pos.astype(jnp.int32).reshape(1)
 
-    fwd_all = lax.all_gather(fwd_keys_values, "tp")
-    bwd_all = lax.all_gather(keys_values, "tp")
+    fwd_all = gather_all(fwd_keys_values)
 
     def to_mirror(chunk, turn, senders):
         route = [
@@ -203,7 +444,7 @@
     fwd_marked = jnp.logical_and(early, flag_pair[0] == 1)
     bwd_marked = jnp.logical_and(early, flag_pair[1] == 1).astype(jnp.int32)
 
-    out = forward_all(position, fwd_query, fwd_all)
+    out, bwd_all = forward_all(fwd_query, fwd_all, keys_values)
     passed = lax.ppermute(out, "section", [(s, s + 1) for s in range(sections - 1)])
     mirror = jnp.zeros((micro, width * rows, columns), out.dtype)
     for turn in range(width):
@@ -221,8 +462,8 @@
             index, position, bwd_marked[index : index + 1], query, bwd_all, grad_out, held
         )
         dqs.append(dquery)
-        grads.append(lax.psum_scatter(partial, "tp", scatter_dimension=0))
-    return (passed[None], jnp.concatenate(dqs)[None], jnp.stack(grads)[None], mirror[None])
+        grads.append(partial)
+    return (passed[None], jnp.concatenate(dqs)[None], scatter_sum(grads)[None], mirror[None])
 
 
 def solution(mesh):

time: 376 us -> 348 us (0.926); the launches traced: 372 us -> 348 us
  Pallas kernels: 60.1 us -> 245 us
  waiting for transfers between devices: 207 us -> 56.3 us
  starting transfers between devices: 63.5 us -> 27.4 us
  between operations: 14.2 us -> 1.32 us
  local copies, waits for them, and re-layouts: 22.4 us -> 14.7 us
    pallas_call x1 -> x3, Pallas kernels: 16.3 us -> 202 us  [the longest x1 104 us: forward_all(): pl.pallas_call(forward_kernel, grid=(micro, kv_count), in_specs=[pl.Block...]
    all_gather x2 -> x0, waiting for transfers between devices: 72.3 us -> none  [the longest x1 41.6 us: per_device(): bwd_all = lax.all_gather(keys_values, 'tp')]
    reduce_scatter x2 -> x0, waiting for transfers between devices: 67 us -> none  [per_device(): grads.append(lax.psum_scatter(partial, 'tp', scatter_dimension=0))]
    ppermute x16, starting transfers between devices: 61.3 us -> 25.5 us  [to_mirror(): return lax.ppermute(chunk, ('section', 'tp'), route)]
    ppermute x16, waiting for transfers between devices: 66.4 us -> 56.3 us  [to_mirror(): return lax.ppermute(chunk, ('section', 'tp'), route)]
    unnamed x22 -> x37, local copies, waits for them, and re-layouts: 18.2 us -> 10.2 us
  transfers between devices with their start and end apart: 21 -> 17, of which waited for: 6 -> 6; matrix products, arithmetic and copies ran while one was open for 4% -> 2% of each run, Pallas kernels for 16% -> 70%
where the time goes in v1:
time: 348 us
  Pallas kernels  245 us (70%)
  waiting for transfers between devices  56.3 us (16%)
  starting transfers between devices  27.4 us (8%)
  local copies, waits for them, and re-layouts  14.7 us (4%)
    pallas_call x1, Pallas kernels, forward_all(): pl.pallas_call(forward_kernel, grid=(micro, kv_count), in_specs=[pl.Block...  104 us
    ppermute x16, waiting for transfers between devices, to_mirror(): return lax.ppermute(chunk, ('section', 'tp'), route)  56.3 us
    pallas_call x1, Pallas kernels, gather_all(): pl.pallas_call(gather_kernel, in_specs=[pl.BlockSpec(memory_space=pl.ANY)...  52.3 us
    pallas_call x1, Pallas kernels, scatter_sum(): pl.pallas_call(scatter_kernel, in_specs=[pl.BlockSpec(memory_space=pltpu....  45.2 us
    pallas_call x2, Pallas kernels, backward_one(): pl.pallas_call(backward_kernel, grid_spec=pltpu.PrefetchScalarGridSpec(nu...  42.9 us
    ppermute x16, starting transfers between devices, to_mirror(): return lax.ppermute(chunk, ('section', 'tp'), route)  25.5 us
    unnamed x37, local copies, waits for them, and re-layouts  10.2 us
  transfers between devices with their start and end apart: 17, of which 6 were waited for; matrix products, arithmetic and copies ran while one was open for 2% of the time, Pallas kernels for 70%

profile of v1, /device:TPU:26, one launch (start us, length us, event | category | flops | bytes accessed | tf_op | source)
XLA Modules:
  0.0 347.5 jit_solution(3846179897306160573)
XLA Ops:
  0.8 2.6 dynamic-slice_bitcast_fusion
  3.4 3.4 collective-permute-start.8
  6.8 2.0 collective-permute-start.6
  8.8 2.0 collective-permute-start.2
  10.8 2.0 collective-permute-start.1
  12.8 52.3 %gather_keys_values.1.k_ref.v_ref = bf16[8,2,2,128,512]{4,3,2,1,0:T(8,128)(2,1)} custom-call(bf16[2,2,128,512]{3,2,1,0:T(8,128)(2,1)} %bitcast.67), custom_call_target="tpu_custom_call" | custom-call | tf_op jit(solution)/shard_map/gather_keys_values/pallas_call | solution.py:160
  65.1 1.6 copy-done.1
  66.7 104.1 %attention_forward.1 = (bf16[2,128,4096]{2,1,0:T(8,128)(2,1)S(1)}, bf16[8,2,2,128,512]{4,3,2,1,0:T(8,128)(2,1)}) custom-call(bf16[2,128,4096]{2,1,0:T(8,128)(2,1)S(1)} %bitcast.63, bf16[8,2,2,128,512]{4,3,2,1,0:T(8,128)(2,1)} %gather_keys_values.1.k_ref.v_ref, bf16[8,2,2,128,512]{4,3,2,1,0:T(8,128)(2,1)} %gather_keys_values.1.k_ref.v_ref, ...), custom_call_target="tpu_custom_call" | custom-call | flops 8589934592 | bytes 12582912 | tf_op jit(solution)/shard_map/attention_forward/pallas_call | solution.py:336
  170.9 1.9 collective-permute-start
  172.9 1.6 dynamic-slice_select_fusion
  175.1 1.6 collective-permute-start.3
  177.7 1.3 collective-permute-start.4
  179.9 3.8 %collective-permute-done.3 = bf16[2,128,512]{2,1,0:T(8,128)(2,1)S(1)} collective-permute-done((bf16[2,128,512]{2,1,0:T(8,128)(2,1)}, bf16[2,128,512]{2,1,0:T(8,128)(2,1)S(1)}, u32[]{:S(2)}, u32[]{:S(2)}) %collective-permute-start.3) | collective-permute-done | bytes 262176 | tf_op jit(solution)/shard_map/ppermute | solution.py:431
  183.7 1.3 collective-permute-start.5
  185.1 4.3 %collective-permute-done.4 = bf16[2,128,512]{2,1,0:T(8,128)(2,1)S(1)} collective-permute-done((bf16[2,128,512]{2,1,0:T(8,128)(2,1)}, bf16[2,128,512]{2,1,0:T(8,128)(2,1)S(1)}, u32[]{:S(2)}, u32[]{:S(2)}) %collective-permute-start.4) | collective-permute-done | bytes 262176 | tf_op jit(solution)/shard_map/ppermute | solution.py:431
  189.4 1.3 collective-permute-start.7
  190.7 4.0 %collective-permute-done.5 = bf16[2,128,512]{2,1,0:T(8,128)(2,1)S(1)} collective-permute-done((bf16[2,128,512]{2,1,0:T(8,128)(2,1)S(1)}, bf16[2,128,512]{2,1,0:T(8,128)(2,1)S(1)}, u32[]{:S(2)}, u32[]{:S(2)}) %collective-permute-start.5) | collective-permute-done | bytes 262176 | tf_op jit(solution)/shard_map/ppermute | solution.py:431
  196.1 1.3 collective-permute-start.15
  198.4 1.3 collective-permute-start.10
  199.7 1.5 collective-permute-start.9
  202.2 1.3 copy-done.13
  203.5 21.4 %attention_backward.3 = (bf16[1,128,4096]{2,1,0:T(8,128)(2,1)S(1)}, bf16[8,2,128,512]{3,2,1,0:T(8,128)(2,1)S(1)}) custom-call(s32[1]{0:T(128)} %bitcast.4.pos_ref, s32[1]{0:T(128)} %bitcast.24.flag_ref, bf16[2,128,4096]{2,1,0:T(8,128)(2,1)S(1)} %bitcast.64, bf16[8,2,2,128,512]{4,3,2,1,0:T(8,128)(2,1)} %get-tuple-element.11.k_ref.v_ref, ...), custom_call_target="tpu_custom_call" | custom-call | flops 10737418240 | bytes 12582912 | tf_op jit(solution)/shard_map/attention_backward/pallas_call | solution.py:378
  224.9 21.5 %attention_backward.2 = (bf16[1,128,4096]{2,1,0:T(8,128)(2,1)S(1)}, bf16[8,2,128,512]{3,2,1,0:T(8,128)(2,1)S(1)}) custom-call(s32[1]{0:T(128)} %bitcast.4.pos_ref, s32[1]{0:T(128)} %bitcast.5.flag_ref, bf16[2,128,4096]{2,1,0:T(8,128)(2,1)S(1)} %bitcast.65, bf16[8,2,2,128,512]{4,3,2,1,0:T(8,128)(2,1)} %get-tuple-element.11.k_ref.v_ref, ...), custom_call_target="tpu_custom_call" | custom-call | flops 10737418240 | bytes 12582912 | tf_op jit(solution)/shard_map/attention_backward/pallas_call | solution.py:378
  246.5 1.4 collective-permute-start.11
  248.1 1.3 collective-permute-start.12
  249.4 17.7 %collective-permute-done.11 = bf16[2,128,512]{2,1,0:T(8,128)(2,1)S(1)} collective-permute-done((bf16[2,128,512]{2,1,0:T(8,128)(2,1)S(1)}, bf16[2,128,512]{2,1,0:T(8,128)(2,1)S(1)}, u32[]{:S(2)}, u32[]{:S(2)}) %collective-permute-start.11) | collective-permute-done | bytes 262176 | tf_op jit(solution)/shard_map/ppermute | solution.py:431
  267.1 1.3 collective-permute-start.13
  268.4 16.4 %collective-permute-done.12 = bf16[2,128,512]{2,1,0:T(8,128)(2,1)S(1)} collective-permute-done((bf16[2,128,512]{2,1,0:T(8,128)(2,1)S(1)}, bf16[2,128,512]{2,1,0:T(8,128)(2,1)S(1)}, u32[]{:S(2)}, u32[]{:S(2)}) %collective-permute-start.12) | collective-permute-done | bytes 262176 | tf_op jit(solution)/shard_map/ppermute | solution.py:431
  286.2 10.0 %collective-permute-done.14 = bf16[2,128,512]{2,1,0:T(8,128)(2,1)S(1)} collective-permute-done((bf16[2,128,512]{2,1,0:T(8,128)(2,1)S(1)}, bf16[2,128,512]{2,1,0:T(8,128)(2,1)S(1)}, u32[]{:S(2)}, u32[]{:S(2)}) %collective-permute-start.14) | collective-permute-done | bytes 262176 | tf_op jit(solution)/shard_map/ppermute | solution.py:431
  296.3 45.2 %scatter_gradients.1 = bf16[2,2,128,512]{3,2,1,0:T(8,128)(2,1)S(1)} custom-call(bf16[8,2,128,512]{3,2,1,0:T(8,128)(2,1)S(1)} %get-tuple-element.14.refs_0_, bf16[8,2,128,512]{3,2,1,0:T(8,128)(2,1)S(1)} %get-tuple-element.15.refs_1_), custom_call_target="tpu_custom_call" | custom-call | tf_op jit(solution)/shard_map/scatter_gradients/pallas_call | solution.py:270
  341.6 1.7 maximum_bitcast_fusion
  343.6 3.1 copy.28
  (60 shorter events, 8.7 us)
Async XLA Ops:
  0.6 172.2 %copy-start = (s32[2,2,2]{2,1,0:T(2,128)S(1)}, s32[2,2,2]{2,1,0:T(2,128)}, u32[]{:S(2)}) copy-start(s32[2,2,2]{2,1,0:T(2,128)} %param.13) | copy-start | bytes 100
  3.4 196.3 %collective-permute-start.8 = (bf16[2,128,512]{2,1,0:T(8,128)(2,1)S(1)}, bf16[2,128,512]{2,1,0:T(8,128)(2,1)}, u32[]{:S(2)}, u32[]{:S(2)}) collective-permute-start(bf16[2,128,512]{2,1,0:T(8,128)(2,1)S(1)} %get-tuple-element.24), channel_id=1, source_target_pairs={{16,15},{17,8},{18,9},{19,10},{20,11},{21,12},{22,13},{23,14},{24,... | collective-permute-start | bytes 786440 | tf_op jit(solution)/shard_map/ppermute | solution.py:431
  6.8 189.3 %collective-permute-start.6 = (bf16[2,128,512]{2,1,0:T(8,128)(2,1)S(1)}, bf16[2,128,512]{2,1,0:T(8,128)(2,1)}, u32[]{:S(2)}, u32[]{:S(2)}) collective-permute-start(bf16[2,128,512]{2,1,0:T(8,128)(2,1)S(1)} %get-tuple-element.25), channel_id=1, source_target_pairs={{16,13},{17,14},{18,15},{19,8},{20,9},{21,10},{22,11},{23,12},{24,... | collective-permute-start | bytes 786440 | tf_op jit(solution)/shard_map/ppermute | solution.py:431
  8.8 168.8 %collective-permute-start.2 = (bf16[2,128,512]{2,1,0:T(8,128)(2,1)}, bf16[2,128,512]{2,1,0:T(8,128)(2,1)}, u32[]{:S(2)}, u32[]{:S(2)}) collective-permute-start(bf16[2,128,512]{2,1,0:T(8,128)(2,1)} %get-tuple-element.29), channel_id=1, source_target_pairs={{16,9},{17,10},{18,11},{19,12},{20,13},{21,14},{22,15},{23,8},{24,... | collective-permute-start | bytes 786440 | tf_op jit(solution)/shard_map/ppermute | solution.py:431
  10.8 164.3 %collective-permute-start.1 = (bf16[2,128,512]{2,1,0:T(8,128)(2,1)}, bf16[2,128,512]{2,1,0:T(8,128)(2,1)}, u32[]{:S(2)}, u32[]{:S(2)}) collective-permute-start(bf16[2,128,512]{2,1,0:T(8,128)(2,1)} %get-tuple-element.30), channel_id=1, source_target_pairs={{16,8},{17,9},{18,10},{19,11},{20,12},{21,13},{22,14},{23,15},{24,... | collective-permute-start | bytes 786440 | tf_op jit(solution)/shard_map/ppermute | solution.py:431
  12.8 52.3 %copy-start.3 = (bf16[1,2,2,128,512]{4,3,2,1,0:T(8,128)(2,1)S(1)}, bf16[1,2,2,128,512]{4,3,2,1,0:T(8,128)(2,1)}, u32[]{:S(2)}) copy-start(bf16[1,2,2,128,512]{4,3,2,1,0:T(8,128)(2,1)} %param.8) | copy-start | bytes 1572868
  65.1 1.6 copy-start.1
  170.9 172.7 %collective-permute-start = (bf16[2,128,4096]{2,1,0:T(8,128)(2,1)S(1)}, bf16[2,128,4096]{2,1,0:T(8,128)(2,1)}, u32[]{:S(2)}, u32[]{:S(2)}) collective-permute-start(bf16[2,128,4096]{2,1,0:T(8,128)(2,1)S(1)} %get-tuple-element.10), channel_id=1, source_target_pairs={{0,8},{8,16},{16,24},{1,9},{9,17},{17,25},{2,10},{10,18},{18,26},{... | collective-permute-start | bytes 6291464 | tf_op jit(solution)/shard_map/ppermute | solution.py:448
  172.9 10.8 %copy-start.5 = (bf16[2,128,512]{2,1,0:T(8,128)(2,1)S(1)}, bf16[2,128,512]{2,1,0:T(8,128)(2,1)}, u32[]{:S(2)}) copy-start(bf16[2,128,512]{2,1,0:T(8,128)(2,1)} %get-tuple-element.26) | copy-start | bytes 786436
  175.1 21.0 %copy-start.6 = (bf16[2,128,512]{2,1,0:T(8,128)(2,1)S(1)}, bf16[2,128,512]{2,1,0:T(8,128)(2,1)}, u32[]{:S(2)}) copy-start(bf16[2,128,512]{2,1,0:T(8,128)(2,1)} %get-tuple-element.17) | copy-start | bytes 786436
  175.1 23.3 %copy-start.11 = (bf16[2,128,512]{2,1,0:T(8,128)(2,1)S(1)}, bf16[2,128,512]{2,1,0:T(8,128)(2,1)}, u32[]{:S(2)}) copy-start(bf16[2,128,512]{2,1,0:T(8,128)(2,1)} %get-tuple-element.22) | copy-start | bytes 786436
  175.1 24.6 %copy-start.12 = (bf16[2,128,512]{2,1,0:T(8,128)(2,1)S(1)}, bf16[2,128,512]{2,1,0:T(8,128)(2,1)}, u32[]{:S(2)}) copy-start(bf16[2,128,512]{2,1,0:T(8,128)(2,1)} %get-tuple-element.23) | copy-start | bytes 786436
  175.1 28.4 %copy-start.2 = (bf16[1,2,128,4096]{3,2,1,0:T(8,128)(2,1)S(1)}, bf16[1,2,128,4096]{3,2,1,0:T(8,128)(2,1)}, u32[]{:S(2)}) copy-start(bf16[1,2,128,4096]{3,2,1,0:T(8,128)(2,1)} %param.7) | copy-start | bytes 6291460
  175.1 8.6 %collective-permute-start.3 = (bf16[2,128,512]{2,1,0:T(8,128)(2,1)}, bf16[2,128,512]{2,1,0:T(8,128)(2,1)S(1)}, u32[]{:S(2)}, u32[]{:S(2)}) collective-permute-start(bf16[2,128,512]{2,1,0:T(8,128)(2,1)} %get-tuple-element.28), channel_id=1, source_target_pairs={{16,10},{17,11},{18,12},{19,13},{20,14},{21,15},{22,8},{23,9},{24,... | collective-permute-start | bytes 786440 | tf_op jit(solution)/shard_map/ppermute | solution.py:431
  177.7 11.7 %collective-permute-start.4 = (bf16[2,128,512]{2,1,0:T(8,128)(2,1)}, bf16[2,128,512]{2,1,0:T(8,128)(2,1)S(1)}, u32[]{:S(2)}, u32[]{:S(2)}) collective-permute-start(bf16[2,128,512]{2,1,0:T(8,128)(2,1)} %get-tuple-element.27), channel_id=1, source_target_pairs={{16,11},{17,12},{18,13},{19,14},{20,15},{21,8},{22,9},{23,10},{24,... | collective-permute-start | bytes 786440 | tf_op jit(solution)/shard_map/ppermute | solution.py:431
  183.7 11.0 %collective-permute-start.5 = (bf16[2,128,512]{2,1,0:T(8,128)(2,1)S(1)}, bf16[2,128,512]{2,1,0:T(8,128)(2,1)S(1)}, u32[]{:S(2)}, u32[]{:S(2)}) collective-permute-start(bf16[2,128,512]{2,1,0:T(8,128)(2,1)S(1)} %copy-done.5), channel_id=1, source_target_pairs={{16,12},{17,13},{18,14},{19,15},{20,8},{21,9},{22,10},{23,11},{24,... | collective-permute-start | bytes 786440 | tf_op jit(solution)/shard_map/ppermute | solution.py:431
  189.4 9.0 %collective-permute-start.7 = (bf16[2,128,512]{2,1,0:T(8,128)(2,1)S(1)}, bf16[2,128,512]{2,1,0:T(8,128)(2,1)S(1)}, u32[]{:S(2)}, u32[]{:S(2)}) collective-permute-start(bf16[2,128,512]{2,1,0:T(8,128)(2,1)S(1)} %get-tuple-element.31), channel_id=1, source_target_pairs={{16,14},{17,15},{18,8},{19,9},{20,10},{21,11},{22,12},{23,13},{24,... | collective-permute-start | bytes 786440 | tf_op jit(solution)/shard_map/ppermute | solution.py:431
  194.7 146.8 %collective-permute-start.16 = (bf16[2,128,512]{2,1,0:T(8,128)(2,1)S(1)}, bf16[2,128,512]{2,1,0:T(8,128)(2,1)S(1)}, u32[]{:S(2)}, u32[]{:S(2)}) collective-permute-start(bf16[2,128,512]{2,1,0:T(8,128)(2,1)S(1)} %get-tuple-element.16), channel_id=1, source_target_pairs={{0,31},{1,24},{2,25},{3,26},{4,27},{5,28},{6,29},{7,30},{8,23},{9,... | collective-permute-start | bytes 786440 | tf_op jit(solution)/shard_map/ppermute | solution.py:431
  196.1 145.4 %collective-permute-start.15 = (bf16[2,128,512]{2,1,0:T(8,128)(2,1)S(1)}, bf16[2,128,512]{2,1,0:T(8,128)(2,1)S(1)}, u32[]{:S(2)}, u32[]{:S(2)}) collective-permute-start(bf16[2,128,512]{2,1,0:T(8,128)(2,1)S(1)} %copy-done.6), channel_id=1, source_target_pairs={{0,30},{1,31},{2,24},{3,25},{4,26},{5,27},{6,28},{7,29},{8,22},{9,... | collective-permute-start | bytes 786440 | tf_op jit(solution)/shard_map/ppermute | solution.py:431
  198.4 49.7 %collective-permute-start.10 = (bf16[2,128,512]{2,1,0:T(8,128)(2,1)S(1)}, bf16[2,128,512]{2,1,0:T(8,128)(2,1)S(1)}, u32[]{:S(2)}, u32[]{:S(2)}) collective-permute-start(bf16[2,128,512]{2,1,0:T(8,128)(2,1)S(1)} %copy-done.11), channel_id=1, source_target_pairs={{0,25},{1,26},{2,27},{3,28},{4,29},{5,30},{6,31},{7,24},{8,17},{9,... | collective-permute-start | bytes 786440 | tf_op jit(solution)/shard_map/ppermute | solution.py:431
  199.7 46.7 %collective-permute-start.9 = (bf16[2,128,512]{2,1,0:T(8,128)(2,1)S(1)}, bf16[2,128,512]{2,1,0:T(8,128)(2,1)S(1)}, u32[]{:S(2)}, u32[]{:S(2)}) collective-permute-start(bf16[2,128,512]{2,1,0:T(8,128)(2,1)S(1)} %copy-done.12), channel_id=1, source_target_pairs={{0,24},{1,25},{2,26},{3,27},{4,28},{5,29},{6,30},{7,31},{8,16},{9,... | collective-permute-start | bytes 786440 | tf_op jit(solution)/shard_map/ppermute | solution.py:431
  202.2 1.3 copy-start.13
  224.9 21.6 %copy-start.10 = (bf16[2,128,512]{2,1,0:T(8,128)(2,1)S(1)}, bf16[2,128,512]{2,1,0:T(8,128)(2,1)}, u32[]{:S(2)}) copy-start(bf16[2,128,512]{2,1,0:T(8,128)(2,1)} %get-tuple-element.21) | copy-start | bytes 786436
  246.4 1.7 copy-start.9
  246.4 20.7 %copy-start.8 = (bf16[2,128,512]{2,1,0:T(8,128)(2,1)S(1)}, bf16[2,128,512]{2,1,0:T(8,128)(2,1)}, u32[]{:S(2)}) copy-start(bf16[2,128,512]{2,1,0:T(8,128)(2,1)} %get-tuple-element.19) | copy-start | bytes 786436
  246.4 38.4 %copy-start.7 = (bf16[2,128,512]{2,1,0:T(8,128)(2,1)S(1)}, bf16[2,128,512]{2,1,0:T(8,128)(2,1)}, u32[]{:S(2)}) copy-start(bf16[2,128,512]{2,1,0:T(8,128)(2,1)} %get-tuple-element.18) | copy-start | bytes 786436
  246.5 20.6 %collective-permute-start.11 = (bf16[2,128,512]{2,1,0:T(8,128)(2,1)S(1)}, bf16[2,128,512]{2,1,0:T(8,128)(2,1)S(1)}, u32[]{:S(2)}, u32[]{:S(2)}) collective-permute-start(bf16[2,128,512]{2,1,0:T(8,128)(2,1)S(1)} %copy-done.10), channel_id=1, source_target_pairs={{0,26},{1,27},{2,28},{3,29},{4,30},{5,31},{6,24},{7,25},{8,18},{9,... | collective-permute-start | bytes 786440 | tf_op jit(solution)/shard_map/ppermute | solution.py:431
  248.1 36.8 %collective-permute-start.12 = (bf16[2,128,512]{2,1,0:T(8,128)(2,1)S(1)}, bf16[2,128,512]{2,1,0:T(8,128)(2,1)S(1)}, u32[]{:S(2)}, u32[]{:S(2)}) collective-permute-start(bf16[2,128,512]{2,1,0:T(8,128)(2,1)S(1)} %copy-done.9), channel_id=1, source_target_pairs={{0,27},{1,28},{2,29},{3,30},{4,31},{5,24},{6,25},{7,26},{8,19},{9,... | collective-permute-start | bytes 786440 | tf_op jit(solution)/shard_map/ppermute | solution.py:431
  267.1 19.1 %collective-permute-start.13 = (bf16[2,128,512]{2,1,0:T(8,128)(2,1)S(1)}, bf16[2,128,512]{2,1,0:T(8,128)(2,1)S(1)}, u32[]{:S(2)}, u32[]{:S(2)}) collective-permute-start(bf16[2,128,512]{2,1,0:T(8,128)(2,1)S(1)} %copy-done.8), channel_id=1, source_target_pairs={{0,28},{1,29},{2,30},{3,31},{4,24},{5,25},{6,26},{7,27},{8,20},{9,... | collective-permute-start | bytes 786440 | tf_op jit(solution)/shard_map/ppermute | solution.py:431
  284.9 11.4 %collective-permute-start.14 = (bf16[2,128,512]{2,1,0:T(8,128)(2,1)S(1)}, bf16[2,128,512]{2,1,0:T(8,128)(2,1)S(1)}, u32[]{:S(2)}, u32[]{:S(2)}) collective-permute-start(bf16[2,128,512]{2,1,0:T(8,128)(2,1)S(1)} %copy-done.7), channel_id=1, source_target_pairs={{0,29},{1,30},{2,31},{3,24},{4,25},{5,26},{6,27},{7,28},{8,21},{9,... | collective-permute-start | bytes 786440 | tf_op jit(solution)/shard_map/ppermute | solution.py:431
  341.6 2.0 copy-start.4
